TPU v7x, 256 devices: a whole 4x4x8 slice. The times are simulated.
256 devices in a mesh: dir: 4 (over x_lo, core), bond: 64 (over y, z, x_hi).
Axes of the slice: x: 4 (x_hi: 2, x_lo: 2; x = x_hi * 2 + x_lo), y: 4, z: 8, core: 2. Of those that a mesh axis runs over, the one named last changes fastest.
Arguments:
- corner_mat: bfloat16 [4, 8192, 8192], P('dir', 'bond'), may hold values from -0.0625 to 0.0625
- edge_mat: bfloat16 [4, 32768, 8192], P('dir', 'bond'), may hold values from -0.0625 to 0.0625
- edge_panel: bfloat16 [4, 8192, 512], P('dir', 'bond'), may hold values from -6 to 6
- vertex_weights: float32 [4, 4, 4], replicated, may hold values from -3 to 3
- projector: bfloat16 [4, 512, 256], P('dir'), may hold values from -0.25 to 0.25
- edge_projector: bfloat16 [4, 8192, 256], P('dir', 'bond'), may hold values from -0.1875 to 0.1875
Outputs:
- new_corner: bfloat16 [4, 32768, 256], P('dir', 'bond')
- gram: float32 [4, 256, 256], P('dir', 'bond')
- new_edge: bfloat16 [4, 256, 512], P('dir', 'bond')
All inputs are finite; a program needn't handle non-finite values.
Results may differ from a plain program's by a relative error of at most 0.0065.
Values may be sent and summed in bfloat16 or wider, within the bound.
No kernel may reach another device: no remote copies, remote signals or barrier semaphores. Data moves between devices by JAX's collectives and lax.ppermute only.
A program may use at most 128 MiB of HBM per device.

v0:
```python
import jax
import jax.numpy as jnp
from jax import lax
from jax.sharding import PartitionSpec as P

CHI = 8192
D = 4
PANEL = 512


def passed_along(block, axis, distance):
    devices = range(lax.axis_size(axis))
    route = [((i - distance) % len(devices), i) for i in devices]
    return lax.ppermute(block, axis, route)


def enlarge(raw_block, vertex_weights):
    row_count = raw_block.shape[0] // D
    split_block = raw_block.reshape(row_count, D, D, PANEL // D)
    mixed_block = jnp.einsum(
        "isub,sut->istb", split_block, vertex_weights, precision=lax.Precision.HIGHEST
    )
    return mixed_block.reshape(row_count * D, PANEL).astype(jnp.bfloat16)


def contract_rows(previous, hidden_panel):
    return jnp.dot(
        previous,
        lax.all_gather(hidden_panel, "bond", axis=0, tiled=True),
        preferred_element_type=jnp.float32,
    )


def build_hidden(corner_rows, panel_rows):
    first_sum = jnp.dot(
        corner_rows,
        lax.all_gather(panel_rows, "bond", axis=0, tiled=True),
        preferred_element_type=jnp.float32,
    )
    return (first_sum,)


def on_device(corner_mat, edge_mat, edge_panel, vertex_weights, projector, edge_projector):
    corner_rows = corner_mat[0]
    own_edge = edge_mat[0]
    panel_rows = edge_panel[0]
    proj_local = projector[0]
    edge_proj_local = edge_projector[0]
    sums = build_hidden(corner_rows, panel_rows)
    new_edge = lax.psum_scatter(
        jnp.dot(edge_proj_local.T, panel_rows, preferred_element_type=jnp.float32),
        "bond",
        scatter_dimension=0,
        tiled=True,
    ).astype(jnp.bfloat16)
    hidden_panel = sums[0].astype(jnp.bfloat16)
    previous = passed_along(own_edge, "dir", 1)
    enlarged = enlarge(contract_rows(previous, hidden_panel), vertex_weights)
    projected = jnp.dot(enlarged, proj_local, preferred_element_type=jnp.float32)
    new_corner = projected.astype(jnp.bfloat16)
    partial_full = jnp.dot(enlarged.T, enlarged, preferred_element_type=jnp.float32)
    gram_slab = lax.psum_scatter(partial_full, "bond", scatter_dimension=0, tiled=True)
    slab_rows = gram_slab.shape[0]
    proj_float = proj_local.astype(jnp.float32)
    right_side = jnp.dot(gram_slab, proj_float, precision=lax.Precision.HIGHEST)
    proj_slab = lax.dynamic_slice_in_dim(
        proj_float, lax.axis_index("bond") * slab_rows, slab_rows, 0
    )
    partial_keep = jnp.dot(proj_slab.T, right_side, precision=lax.Precision.HIGHEST)
    gram = lax.psum_scatter(partial_keep, "bond", scatter_dimension=0, tiled=True) / (CHI * D)
    return (new_corner[None], gram[None], new_edge[None])


def solution(mesh):
    in_specs = (
        P("dir", "bond", None),
        P("dir", "bond", None),
        P("dir", "bond", None),
        P(),
        P("dir", None, None),
        P("dir", "bond", None),
    )
    out_specs = (P("dir", "bond", None), P("dir", "bond", None), P("dir", "bond", None))
    return jax.shard_map(
        on_device, mesh=mesh, in_specs=in_specs, out_specs=out_specs, check_vma=False
    )
```

profile of v0, /device:TPU:2, one launch (start us, length us, event | category | flops | bytes accessed | tf_op | source)
XLA Modules:
  0.0 1349.1 jit_solution(14154525090122535802)
XLA Ops:
  7.2 0.0 copy-start
  7.2 0.0 all-gather.6.cloned.1.call-start
  7.2 0.7 all-gather.6.cloned.1.call-update
  7.9 0.0 all-gather.4.cloned.1.call-start
  8.0 156.1 %all-gather.6.cloned.1.call-done = bf16[1,8192,512]{2,1,0:T(8,128)(2,1)} async-done(((bf16[1,128,512]{2,1,0:T(8,128)(2,1)}), bf16[1,8192,512]{2,1,0:T(8,128)(2,1)}) %all-gather.6.cloned.1.call-update) | async-done | bytes 8388624 | tf_op jit(solution)/shard_map/all_gather | solution.py:37
  164.1 0.0 copy-done
  164.1 5.3 fusion.5
  169.4 0.0 all-gather.4.cloned.1.call-update
  169.4 0.0 reduce-scatter.2.cloned.1.call-start
  169.5 0.0 copy-start.3
  169.5 0.1 collective-permute-start
  169.6 116.7 %collective-permute-done = bf16[512,8192]{1,0:T(8,128)(2,1)} collective-permute-done((bf16[512,8192]{1,0:T(8,128)(2,1)}, bf16[512,8192]{1,0:T(8,128)(2,1)}, u32[]{:S(2)}, u32[]{:S(2)}) %collective-permute-start) | collective-permute-done | bytes 8388640 | tf_op jit(solution)/shard_map/ppermute | solution.py:14
  286.2 38.8 %all-gather.4.cloned.1.call-done = bf16[8192,512]{1,0:T(8,128)(2,1)} async-done(((bf16[128,512]{1,0:T(8,128)(2,1)}), bf16[8192,512]{1,0:T(8,128)(2,1)}) %all-gather.4.cloned.1.call-update) | async-done | bytes 8388624 | tf_op jit(solution)/shard_map/all_gather | solution.py:29
  325.0 11.3 convolution_bitcast_fusion
  336.3 0.0 copy-start.1
  336.3 0.0 copy-start.2
  336.3 0.0 copy-start.4
  336.3 1.6 copy.15
  337.9 1.3 reshape.14
  339.2 0.0 copy-done.3
  339.2 3.1 fusion.3
  342.4 0.2 copy.18
  342.6 1.4 fusion.11
  344.0 0.0 reduce-scatter.2.cloned.1.call-update
  344.0 0.0 all-reduce.5.cloned.1.call-start
  344.1 0.0 copy-done.1
  344.1 0.0 copy-done.2
  344.1 0.2 fusion.19
  344.4 0.0 copy-done.4
  344.4 0.6 dynamic-slice.1
  345.6 360.8 %all-reduce.6 = bf16[256,512]{1,0:T(8,128)(2,1)S(1)} all-reduce(f32[256,512]{1,0:T(8,128)S(1)} %fusion.19), channel_id=5, replica_groups=mesh['dir'=4,'bond'=64] {'bond'}, use_global_device_ids=true, to_apply=%region_2.0.clone | all-reduce | flops 131072 | bytes 786432
  706.4 1.1 reduce-scatter.2.cloned.1.call-done
  707.5 1.1 fusion.16
  708.7 1.8 fusion.25
  710.4 0.0 all-reduce.5.cloned.1.call-update
  710.4 0.6 fusion.23
  711.0 1.9 fusion.4
  713.0 628.3 %all-reduce.5.cloned.1.call-done = f32[256,256]{1,0:T(8,128)} async-done(((f32[256,256]{1,0:T(8,128)}), f32[256,256]{1,0:T(8,128)}) %all-reduce.5.cloned.1.call-update) | async-done | bytes 262160
  1341.3 1.3 fusion.24
Async XLA Ops:
  7.2 156.9 %copy-start = (bf16[1,128,8192]{2,1,0:T(8,128)(2,1)S(1)}, bf16[1,128,8192]{2,1,0:T(8,128)(2,1)}, u32[]{:S(2)}) copy-start(bf16[1,128,8192]{2,1,0:T(8,128)(2,1)} %param.6) | copy-start | bytes 6291460
  7.2 156.9 %all-gather.6.cloned.1.call-start = ((), (), s32[]{:S(2)}) async-start(), calls=%async_computation.3 | async-start | bytes 8519680 | tf_op jit(solution)/shard_map/all_gather | solution.py:37
  7.9 317.1 %all-gather.4.cloned.1.call-start = ((), (), s32[]{:S(2)}) async-start(), calls=%async_computation.1 | async-start | bytes 8519680 | tf_op jit(solution)/shard_map/all_gather | solution.py:29
  169.4 538.1 %reduce-scatter.2.cloned.1.call-start = ((), (), s32[]{:S(2)}) async-start(), calls=%async_computation.2 | async-start | bytes 1064960 | tf_op jit(solution)/shard_map/reduce_scatter | solution.py:62
  169.5 169.7 %copy-start.3 = (f32[4,4,4]{2,1,0:T(4,128)S(1)}, f32[4,4,4]{2,1,0:T(4,128)}, u32[]{:S(2)}) copy-start(f32[4,4,4]{2,1,0:T(4,128)} %param.9) | copy-start | bytes 772
  169.5 116.8 %collective-permute-start = (bf16[512,8192]{1,0:T(8,128)(2,1)}, bf16[512,8192]{1,0:T(8,128)(2,1)}, u32[]{:S(2)}, u32[]{:S(2)}) collective-permute-start(bf16[512,8192]{1,0:T(8,128)(2,1)} %bitcast.54), channel_id=1, source_target_pairs={{192,0},{0,64},{64,128},{128,192},{193,1},{1,65},{65,129},{129,193... | collective-permute-start | bytes 25165832 | tf_op jit(solution)/shard_map/ppermute | solution.py:14
  336.3 7.8 copy-start.1
  336.3 7.8 copy-start.2
  336.3 8.1 copy-start.4
  344.0 997.3 %all-reduce.5.cloned.1.call-start = ((), (), s32[]{:S(2)}) async-start(), calls=%async_computation.4 | async-start | bytes 524288
Sparse Core Ops, SparseCore 0:
  11.5 152.5 all-gather.5
  169.5 155.4 all-gather.3
  344.1 363.3 reduce-scatter.1
  710.6 630.6 all-reduce.4
where the time goes:
time: 1350 us
  waiting for transfers between devices  942 us (70%)
  blocking collectives  361 us (27%)
  matrix products  26.2 us (2%)
  between operations  14.5 us (1%)
    unnamed x5, waiting for transfers between devices  629 us
    unnamed x1, blocking collectives  361 us
    all_gather x1, waiting for transfers between devices, build_hidden(): lax.all_gather(panel_rows, 'bond', axis=0, tiled=True)  156 us
    ppermute x1, waiting for transfers between devices, passed_along(): return lax.ppermute(block, axis, route)  117 us
    all_gather x1, waiting for transfers between devices, contract_rows(): lax.all_gather(hidden_panel, 'bond', axis=0, tiled=True)  38.8 us
  transfers between devices with their start and end apart: 5, of which 5 were waited for; matrix products, arithmetic and copies ran while one was open for 0% of the time, Pallas kernels for 0%

commit v1 on v0

v1 whole, which is shorter than its diff:
```python
import jax
import jax.numpy as jnp
from jax import lax
from jax.sharding import PartitionSpec as P

CHI = 8192
D = 4
PANEL = 512
KEEP = 256


def passed_along(block, axis, distance):
    devices = range(lax.axis_size(axis))
    route = [((i - distance) % len(devices), i) for i in devices]
    return lax.ppermute(block, axis, route)


def enlarge(raw_block, vertex_weights):
    row_count = raw_block.shape[0] // D
    split_block = raw_block.reshape(row_count, D, D, PANEL // D)
    mixed_block = jnp.einsum(
        "isub,sut->istb", split_block, vertex_weights, precision=lax.Precision.HIGHEST
    )
    return mixed_block.reshape(row_count * D, PANEL).astype(jnp.bfloat16)


def on_device(corner_mat, edge_mat, edge_panel, vertex_weights, projector, edge_projector):
    corner_rows = corner_mat[0]
    own_edge = edge_mat[0]
    panel_rows = edge_panel[0]
    proj_next = passed_along(projector[0], "dir", -1)
    edge_proj_rows = lax.all_to_all(
        edge_projector[0].T, "bond", split_axis=0, concat_axis=1, tiled=True
    )
    panel_full = lax.all_gather(panel_rows, "bond", axis=0, tiled=True)
    hidden_panel = jnp.dot(
        corner_rows, panel_full, preferred_element_type=jnp.float32
    ).astype(jnp.bfloat16)
    hidden_full = lax.all_gather(
        passed_along(hidden_panel, "dir", -1), "bond", axis=0, tiled=True
    )
    new_edge = jnp.dot(
        edge_proj_rows, panel_full, preferred_element_type=jnp.float32
    ).astype(jnp.bfloat16)
    raw_block = jnp.dot(own_edge, hidden_full, preferred_element_type=jnp.float32)
    enlarged = enlarge(raw_block, vertex_weights)
    projected = jnp.dot(enlarged, proj_next, preferred_element_type=jnp.float32)
    new_corner = passed_along(projected.astype(jnp.bfloat16), "dir", 1)
    partial_gram = jnp.dot(projected.T, projected, precision=lax.Precision.HIGHEST)
    partials = lax.all_to_all(partial_gram, "bond", split_axis=0, concat_axis=0, tiled=True)
    gram = partials.reshape(lax.axis_size("bond"), -1, KEEP).sum(axis=0) / (CHI * D)
    gram = passed_along(gram, "dir", 1)
    return (new_corner[None], gram[None], new_edge[None])


def solution(mesh):
    in_specs = (
        P("dir", "bond", None),
        P("dir", "bond", None),
        P("dir", "bond", None),
        P(),
        P("dir", None, None),
        P("dir", "bond", None),
    )
    out_specs = (P("dir", "bond", None), P("dir", "bond", None), P("dir", "bond", None))
    return jax.shard_map(
        on_device, mesh=mesh, in_specs=in_specs, out_specs=out_specs, check_vma=False
    )
```

time: 1350 us -> 393 us (0.29)
  waiting for transfers between devices: 942 us -> 330 us
  blocking collectives: 361 us -> 0 us
  starting transfers between devices: 0.24 us -> 16.7 us
    unnamed x5 -> x2, waiting for transfers between devices: 629 us -> 0.7 us
    unnamed x1 -> x0, blocking collectives: 361 us -> none
    ppermute x1 -> x4, waiting for transfers between devices: 117 us -> 2.52 us  [passed_along(): return lax.ppermute(block, axis, route)]
    all_gather x2, waiting for transfers between devices: 195 us -> 303 us  [the longest x1 156 us: on_device(): panel_full = lax.all_gather(panel_rows, 'bond', axis=0, tiled=True)]
    all_to_all x0 -> x2, waiting for transfers between devices: none -> 23.6 us  [the longest x1 11.9 us: on_device(): lax.all_to_all(partial_gram, 'bond', split_axis=0, concat_axis=0, tiled=T...]
    all_to_all x0 -> x2, starting transfers between devices: none -> 14.5 us  [the longest x1 8.98 us: on_device(): lax.all_to_all(partial_gram, 'bond', split_axis=0, concat_axis=0, tiled=T...]
  transfers between devices with their start and end apart: 5 -> 8, of which waited for: 5 -> 5; matrix products, arithmetic and copies ran while one was open for 0% -> 6% of each run, Pallas kernels for 0% -> 0%
where the time goes in v1:
time: 393 us
  waiting for transfers between devices  330 us (84%)
  matrix products  25.6 us (7%)
  starting transfers between devices  16.7 us (4%)
  between operations  14.2 us (4%)
  local copies, waits for them, and re-layouts  6.64 us (2%)
    all_gather x1, waiting for transfers between devices, on_device(): panel_full = lax.all_gather(panel_rows, 'bond', axis=0, tiled=True)  156 us
    all_gather x1, waiting for transfers between devices, on_device(): lax.all_gather(passed_along(hidden_panel, 'dir', -1), 'bond', axis=0, til...  147 us
    all_to_all x1, waiting for transfers between devices, on_device(): lax.all_to_all(partial_gram, 'bond', split_axis=0, concat_axis=0, tiled=T...  11.9 us
    all_to_all x1, waiting for transfers between devices, on_device(): lax.all_to_all(edge_projector[0].T, 'bond', split_axis=0, concat_axis=1,...  11.8 us
    dot_general x1, matrix products, on_device(): jnp.dot(own_edge, hidden_full, preferred_element_type=jnp.float32)  11.3 us
    all_to_all x1, starting transfers between devices, on_device(): lax.all_to_all(partial_gram, 'bond', split_axis=0, concat_axis=0, tiled=T...  8.98 us
  transfers between devices with their start and end apart: 8, of which 5 were waited for; matrix products, arithmetic and copies ran while one was open for 6% of the time, Pallas kernels for 0%

profile of v1, /device:TPU:2, one launch (start us, length us, event | category | flops | bytes accessed | tf_op | source)
XLA Modules:
  0.0 393.1 jit_solution(10095583812295115138)
XLA Ops:
  7.2 0.0 copy-start
  7.2 0.0 all-gather.6.cloned.1.call-start
  7.2 0.7 all-gather.6.cloned.1.call-update
  7.9 0.0 all-gather.4.cloned.1.call-start
  8.0 156.1 %all-gather.6.cloned.1.call-done = bf16[1,8192,512]{2,1,0:T(8,128)(2,1)} async-done(((bf16[1,128,512]{2,1,0:T(8,128)(2,1)}), bf16[1,8192,512]{2,1,0:T(8,128)(2,1)}) %all-gather.6.cloned.1.call-update) | async-done | bytes 8388624 | tf_op jit(solution)/shard_map/all_gather | solution.py:35
  164.1 0.0 copy-done
  164.1 4.6 %fusion.11 = bf16[128,512]{1,0:T(8,128)(2,1)S(1)} fusion(bf16[1,8192,512]{2,1,0:T(8,128)(2,1)} %all-gather.6.cloned.1.call-done, bf16[1,128,8192]{2,1,0:T(8,128)(2,1)S(1)} %copy-done), kind=kOutput, calls=%fused_computation.10 | convolution fusion | flops 1073807360 | bytes 10616832 | tf_op jit(solution)/shard_map/dot_general | solution.py:36
  168.8 0.1 collective-permute-start
  168.8 2.5 collective-permute-done
  171.4 0.0 copy-start.1
  171.4 0.7 copy-done.1
  172.0 0.0 all-gather.4.cloned.1.call-update
  172.0 0.0 copy-start.3
  172.1 1.9 collective-permute-start.1
  174.0 147.0 %all-gather.4.cloned.1.call-done = bf16[8192,512]{1,0:T(8,128)(2,1)} async-done(((bf16[128,512]{1,0:T(8,128)(2,1)}), bf16[8192,512]{1,0:T(8,128)(2,1)}) %all-gather.4.cloned.1.call-update) | async-done | bytes 8388624 | tf_op jit(solution)/shard_map/all_gather | solution.py:39
  321.0 11.3 %fusion.7 = f32[512,512]{0,1:T(8,128)} fusion(bf16[8192,512]{1,0:T(8,128)(2,1)} %all-gather.4.cloned.1.call-done, bf16[1,512,8192]{2,1,0:T(8,128)(2,1)} %param.7), kind=kOutput, calls=%fused_computation.7 | convolution fusion | flops 4294967296 | bytes 17825792 | tf_op jit(solution)/shard_map/dot_general | solution.py:45
  332.3 0.0 copy-start.2
  332.3 1.6 copy.11
  333.9 1.4 reshape.18
  335.3 0.0 copy-done.3
  335.3 3.1 fusion.10
  338.4 0.2 copy.14
  338.6 0.0 collective-permute-done.1
  338.6 0.3 fusion.28
  338.9 1.0 fusion.29
  340.0 0.8 all_to_all.20
  340.8 9.0 %all-to-all-start = ((f32[64,4,256]{2,1,0:T(4,128)}), f32[64,4,256]{2,1,0:T(4,128)S(1)}, u32[]{:S(2)}, u32[]{:S(2)}) async-start(f32[64,4,256]{2,1,0:T(4,128)} %all_to_all.20), calls=%async_computation | async-start | bytes 524288 | tf_op jit(solution)/shard_map/all_to_all | solution.py:50
  349.7 0.0 copy-done.2
  349.8 0.7 copy.15
  350.5 0.0 collective-permute-start.2
  350.5 11.9 %all-to-all-done = f32[64,4,256]{2,1,0:T(4,128)S(1)} async-done(((f32[64,4,256]{2,1,0:T(4,128)}), f32[64,4,256]{2,1,0:T(4,128)S(1)}, u32[]{:S(2)}, u32[]{:S(2)}) %all-to-all-start) | async-done | bytes 262176 | tf_op jit(solution)/shard_map/all_to_all | solution.py:50
  362.3 5.5 %all-to-all-start.1 = ((bf16[64,4,128]{2,1,0:T(4,128)(2,1)}), bf16[64,4,128]{2,1,0:T(4,128)(2,1)S(1)}, u32[]{:S(2)}, u32[]{:S(2)}) async-start(bf16[64,4,128]{2,1,0:T(4,128)(2,1)} %bitcast.11), calls=%async_computation.1 | async-start | bytes 131072 | tf_op jit(solution)/shard_map/all_to_all | solution.py:32
  367.9 0.1 reduce_sum.9
  368.0 0.1 collective-permute-start.3
  368.1 11.8 %all-to-all-done.1 = bf16[64,4,128]{2,1,0:T(4,128)(2,1)S(1)} async-done(((bf16[64,4,128]{2,1,0:T(4,128)(2,1)}), bf16[64,4,128]{2,1,0:T(4,128)(2,1)S(1)}, u32[]{:S(2)}, u32[]{:S(2)}) %all-to-all-start.1) | async-done | bytes 65568 | tf_op jit(solution)/shard_map/all_to_all | solution.py:32
  379.8 5.2 %fusion.19 = bf16[1,4,512]{2,1,0:T(4,128)(2,1)} fusion(bf16[1,8192,512]{2,1,0:T(8,128)(2,1)} %all-gather.6.cloned.1.call-done, bf16[64,4,128]{2,1,0:T(4,128)(2,1)S(1)} %all-to-all-done.1), kind=kOutput, calls=%fused_computation.12 | convolution fusion | flops 33556480 | bytes 8458240 | tf_op jit(solution)/shard_map/dot_general | solution.py:42
  385.0 0.0 collective-permute-done.2
  385.0 0.0 collective-permute-done.3
  385.0 0.7 copy.30
  385.7 0.6 copy.31
  (1 shorter events, 0.0 us)
Async XLA Ops:
  7.2 156.9 %copy-start = (bf16[1,128,8192]{2,1,0:T(8,128)(2,1)S(1)}, bf16[1,128,8192]{2,1,0:T(8,128)(2,1)}, u32[]{:S(2)}) copy-start(bf16[1,128,8192]{2,1,0:T(8,128)(2,1)} %param.6) | copy-start | bytes 6291460
  7.2 156.9 %all-gather.6.cloned.1.call-start = ((), (), s32[]{:S(2)}) async-start(), calls=%async_computation.3 | async-start | bytes 8519680 | tf_op jit(solution)/shard_map/all_gather | solution.py:35
  7.9 313.1 %all-gather.4.cloned.1.call-start = ((), (), s32[]{:S(2)}) async-start(), calls=%async_computation.2 | async-start | bytes 8519680 | tf_op jit(solution)/shard_map/all_gather | solution.py:39
  168.8 2.6 collective-permute-start
  171.4 0.7 copy-start.1
  172.0 163.2 %copy-start.3 = (f32[4,4,4]{2,1,0:T(4,128)S(1)}, f32[4,4,4]{2,1,0:T(4,128)}, u32[]{:S(2)}) copy-start(f32[4,4,4]{2,1,0:T(4,128)} %param.9) | copy-start | bytes 772
  172.1 166.6 %collective-permute-start.1 = (bf16[512,256]{1,0:T(8,128)(2,1)}, bf16[512,256]{1,0:T(8,128)(2,1)S(1)}, u32[]{:S(2)}, u32[]{:S(2)}) collective-permute-start(bf16[512,256]{1,0:T(8,128)(2,1)} %bitcast.6), channel_id=1, source_target_pairs={{64,0},{128,64},{192,128},{0,192},{65,1},{129,65},{193,129},{1,193... | collective-permute-start | bytes 786440 | tf_op jit(solution)/shard_map/ppermute | solution.py:15
  332.3 17.5 %copy-start.2 = (bf16[1,128,256]{2,1,0:T(8,128)(2,1)S(1)}, bf16[1,128,256]{2,1,0:T(8,128)(2,1)}, u32[]{:S(2)}) copy-start(bf16[1,128,256]{2,1,0:T(8,128)(2,1)} %param.11) | copy-start | bytes 196612
  340.8 21.6 %all-to-all-start = ((f32[64,4,256]{2,1,0:T(4,128)}), f32[64,4,256]{2,1,0:T(4,128)S(1)}, u32[]{:S(2)}, u32[]{:S(2)}) async-start(f32[64,4,256]{2,1,0:T(4,128)} %all_to_all.20), calls=%async_computation | async-start | bytes 524288 | tf_op jit(solution)/shard_map/all_to_all | solution.py:50
  350.5 34.5 %collective-permute-start.2 = (bf16[512,256]{1,0:T(8,128)(2,1)S(1)}, bf16[512,256]{1,0:T(8,128)(2,1)S(1)}, u32[]{:S(2)}, u32[]{:S(2)}) collective-permute-start(bf16[512,256]{1,0:T(8,128)(2,1)S(1)} %get-tuple-element.3), channel_id=1, source_target_pairs={{192,0},{0,64},{64,128},{128,192},{193,1},{1,65},{65,129},{129,193... | collective-permute-start | bytes 786440 | tf_op jit(solution)/shard_map/ppermute | solution.py:15
  362.3 17.5 %all-to-all-start.1 = ((bf16[64,4,128]{2,1,0:T(4,128)(2,1)}), bf16[64,4,128]{2,1,0:T(4,128)(2,1)S(1)}, u32[]{:S(2)}, u32[]{:S(2)}) async-start(bf16[64,4,128]{2,1,0:T(4,128)(2,1)} %bitcast.11), calls=%async_computation.1 | async-start | bytes 131072 | tf_op jit(solution)/shard_map/all_to_all | solution.py:32
  368.0 17.0 %collective-permute-start.3 = (f32[4,256]{1,0:T(4,128)S(1)}, f32[4,256]{1,0:T(4,128)S(1)}, u32[]{:S(2)}, u32[]{:S(2)}) collective-permute-start(f32[4,256]{1,0:T(4,128)S(1)} %broadcast_multiply_fusion), channel_id=1, source_target_pairs={{192,0},{0,64},{64,128},{128,192},{193,1},{1,65},{65,129},{129,193... | collective-permute-start | bytes 12296 | tf_op jit(solution)/shard_map/ppermute | solution.py:15
Sparse Core Ops, SparseCore 0:
  11.5 152.5 all-gather.5
  172.2 148.7 all-gather.3
